TPU v7x, 32 devices: a whole 2x2x4 slice. The times are simulated.
32 devices in a mesh: row: 4 (over y, core), col: 4 (over z), depth: 2 (over x).
Axes of the slice: x: 2, y: 2, z: 4, core: 2. Of those that a mesh axis runs over, the one named last changes fastest.
Arguments:
- tokens: bfloat16 [4096, 2048], P(('depth', 'row'), 'col'), may hold values from -6 to 6
- w_in: bfloat16 [8192, 2048], P('col', 'row'), may hold values from -0.125 to 0.125
- w_out: bfloat16 [2048, 8192], P('row', 'col'), may hold values from -0.0625 to 0.0625
- grad_out: bfloat16 [4096, 2048], P(('depth', 'row'), 'col'), may hold values from -6 to 6
Outputs:
- output: bfloat16 [4096, 2048], P(('depth', 'row'), 'col')
- grad_tokens: bfloat16 [4096, 2048], P(('depth', 'row'), 'col')
- grad_w_in: bfloat16 [8192, 2048], P('col', 'row')
- grad_w_out: bfloat16 [2048, 8192], P('row', 'col')
All inputs are finite; a program needn't handle non-finite values.
Results may differ from a plain program's by a relative error of at most 0.005.
Values may be sent and summed in bfloat16 or wider, within the bound.
A program may use at most 192 MiB of HBM per device.

v0:
```python
import math

import jax
import jax.numpy as jnp
from jax import lax
from jax.sharding import PartitionSpec as P


def gelu_value(pre):
    return 0.5 * pre * (1.0 + lax.erf(pre / math.sqrt(2.0)))


def gelu_slope(pre):
    return 0.5 * (1.0 + lax.erf(pre / math.sqrt(2.0))) + pre * jnp.exp(
        -0.5 * pre * pre
    ) / math.sqrt(2.0 * math.pi)


def contract_first(left, right):
    return lax.dot_general(
        left, right, (((0,), (0,)), ((), ())), preferred_element_type=jnp.float32
    )


def contract_last(left, right):
    return lax.dot_general(
        left, right, (((1,), (1,)), ((), ())), preferred_element_type=jnp.float32
    )


def local(tokens, w_in, w_out, grad_out):
    local_rows = tokens.shape[0]
    hidden_local = w_in.shape[0]
    tok_all, cot_all = (
        lax.all_gather(tokens, "col", axis=1, tiled=True),
        lax.all_gather(grad_out, "col", axis=1, tiled=True),
    )
    win_all, wout_all = (
        lax.all_gather(w_in, "row", axis=1, tiled=True),
        lax.all_gather(w_out, "row", axis=0, tiled=True),
    )
    pre = contract_last(tok_all, win_all)
    act = gelu_value(pre).astype(jnp.bfloat16)
    out_term = contract_last(act, wout_all)
    output = lax.psum_scatter(out_term, "col", scatter_dimension=1, tiled=True).astype(jnp.bfloat16)
    d_act = jnp.dot(cot_all, wout_all, preferred_element_type=jnp.float32)
    d_pre = (d_act * gelu_slope(pre)).astype(jnp.bfloat16)
    back_term = jnp.dot(d_pre, win_all, preferred_element_type=jnp.float32)
    grad_tokens = lax.psum_scatter(back_term, "col", scatter_dimension=1, tiled=True).astype(
        jnp.bfloat16
    )
    total_tokens = local_rows * lax.axis_size("row") * lax.axis_size("depth")
    factor = 1.0 / math.sqrt(total_tokens)
    summed = lax.psum_scatter(
        jnp.concatenate([contract_first(cot_all, act), contract_first(tok_all, d_pre)], axis=1),
        ("row", "depth"),
        scatter_dimension=0,
        tiled=True,
    )
    finished = (summed * factor).astype(jnp.bfloat16)
    whole = lax.all_gather(finished, "depth", axis=0, tiled=True)
    grad_w_out = whole[:, :hidden_local]
    grad_w_in = whole[:, hidden_local:].T
    return (output, grad_tokens, grad_w_in, grad_w_out)


def solution(mesh):
    in_specs = (
        P(("depth", "row"), "col"),
        P("col", "row"),
        P("row", "col"),
        P(("depth", "row"), "col"),
    )
    out_specs = (
        P(("depth", "row"), "col"),
        P(("depth", "row"), "col"),
        P("col", "row"),
        P("row", "col"),
    )
    return jax.shard_map(local, mesh=mesh, in_specs=in_specs, out_specs=out_specs, check_vma=False)
```

profile of v0, /device:TPU:0, one launch (start us, length us, event | category | flops | bytes accessed | tf_op | source)
XLA Modules:
  0.0 689.1 jit_solution(5548555696304510300)
XLA Ops:
  7.2 0.0 all-gather.6.cloned.1.call-start
  7.2 0.7 all-gather.6.cloned.1.call-update
  7.9 0.0 all-gather.8.cloned.1.call-start
  7.9 0.7 all-gather.8.cloned.1.call-update
  8.6 0.0 all-gather.12.cloned.1.call-start
  8.7 0.7 all-gather.12.cloned.1.call-update
  9.4 0.0 all-gather.10.cloned.1.call-start
  9.4 0.5 all-gather.10.cloned.1.call-update
  10.0 0.0 reduce-scatter.8.cloned.1.call-start
  10.0 48.2 %all-gather.6.cloned.1.call-done = bf16[512,2048]{1,0:T(8,128)(2,1)} async-done(((bf16[512,512]{1,0:T(8,128)(2,1)}), bf16[512,2048]{1,0:T(8,128)(2,1)}) %all-gather.6.cloned.1.call-update) | async-done | bytes 2097168 | tf_op jit(solution)/shard_map/all_gather | solution.py:35
  58.2 58.6 %all-gather.8.cloned.1.call-done = bf16[2048,2048]{1,0:T(8,128)(2,1)} async-done(((bf16[2048,512]{1,0:T(8,128)(2,1)}), bf16[2048,2048]{1,0:T(8,128)(2,1)}) %all-gather.8.cloned.1.call-update) | async-done | bytes 8388624 | tf_op jit(solution)/shard_map/all_gather | solution.py:39
  116.8 10.5 %fusion.8 = f32[512,2048]{1,0:T(8,128)} fusion(bf16[512,2048]{1,0:T(8,128)(2,1)} %all-gather.6.cloned.1.call-done, bf16[2048,2048]{1,0:T(8,128)(2,1)} %all-gather.8.cloned.1.call-done), kind=kOutput, calls=%fused_computation.16 | convolution fusion | flops 4294967296 | bytes 14680064 | tf_op jit(solution)/shard_map/dot_general | solution.py:26
  127.4 37.0 %all-gather.12.cloned.1.call-done = bf16[512,2048]{1,0:T(8,128)(2,1)} async-done(((bf16[512,512]{1,0:T(8,128)(2,1)}), bf16[512,2048]{1,0:T(8,128)(2,1)}) %all-gather.12.cloned.1.call-update) | async-done | bytes 2097168 | tf_op jit(solution)/shard_map/all_gather | solution.py:36
  164.4 0.0 copy-start
  164.4 15.1 %convolution_bitcast_fusion.1 = f32[2048,2048]{0,1:T(8,128)} fusion(bf16[512,2048]{1,0:T(8,128)(2,1)} %all-gather.12.cloned.1.call-done, f32[512,2048]{1,0:T(8,128)} %fusion.8), kind=kOutput, calls=%fused_computation.2 | convolution fusion | flops 4300210176 | bytes 23068672 | tf_op jit(solution)/shard_map/dot_general | solution.py:20
  179.5 43.3 %all-gather.10.cloned.1.call-done = bf16[2048,2048]{1,0:T(8,128)(2,1)} async-done(((bf16[512,2048]{1,0:T(8,128)(2,1)}), bf16[2048,2048]{1,0:T(8,128)(2,1)}) %all-gather.10.cloned.1.call-update) | async-done | bytes 8388624 | tf_op jit(solution)/shard_map/all_gather | solution.py:40
  222.8 0.0 copy-done
  222.8 0.0 slice-start
  222.8 0.0 slice-start.1
  222.8 0.0 slice-start.2
  222.9 10.8 %fusion.5 = bf16[512,2048]{1,0:T(8,128)(2,1)} fusion(f32[512,2048]{1,0:T(8,128)} %fusion.8, bf16[512,2048]{1,0:T(8,128)(2,1)S(1)} %copy-done, bf16[2048,2048]{1,0:T(8,128)(2,1)} %all-gather.10.cloned.1.call-done), kind=kOutput, calls=%fused_computation.9 | convolution fusion | flops 4305453056 | bytes 16777216 | tf_op jit(solution)/shard_map/dot_general | solution.py:46
  233.6 0.0 slice-start.3
  233.6 7.1 %convolution_bitcast_fusion = f32[2048,2048]{0,1:T(8,128)S(1)} fusion(bf16[512,2048]{1,0:T(8,128)(2,1)} %fusion.5, bf16[512,2048]{1,0:T(8,128)(2,1)} %all-gather.6.cloned.1.call-done), kind=kOutput, calls=%fused_computation.1 | convolution fusion | flops 4294967296 | bytes 20971520 | tf_op jit(solution)/shard_map/dot_general | solution.py:20
  240.7 0.0 slice-done
  240.7 0.0 slice-done.1
  240.8 0.0 slice-done.2
  240.8 0.0 slice-done.3
  240.8 11.9 %pad_maximum_fusion = f32[2048,4096]{0,1:T(8,128)} fusion(f32[2048,2048]{0,1:T(8,128)S(1)} %convolution_bitcast_fusion, f32[2048,2048]{0,1:T(8,128)S(1)} %bitcast.17), kind=kLoop, calls=%fused_computation | loop fusion | flops 8388608 | bytes 67108864 | tf_op jit(solution)/shard_map/concatenate | solution.py:55
  252.6 0.0 copy-start.1
  252.6 0.0 reduce-scatter.8.cloned.1.call-update
  252.7 0.0 reduce-scatter.6.cloned.1.call-start
  252.7 1.5 copy-done.1
  254.2 9.4 %fusion.9 = f32[512,2048]{1,0:T(8,128)} fusion(bf16[512,2048]{1,0:T(8,128)(2,1)S(1)} %copy-done.1, bf16[2048,2048]{1,0:T(8,128)(2,1)} %all-gather.8.cloned.1.call-done), kind=kOutput, calls=%fused_computation.17 | convolution fusion | flops 4294967296 | bytes 14680064 | tf_op jit(solution)/shard_map/dot_general | solution.py:48
  263.7 0.0 reduce-scatter.6.cloned.1.call-update
  263.7 0.3 reduce-scatter.4.cloned.1.call-start
  264.0 13.7 %fusion.6 = f32[512,2048]{1,0:T(8,128)} fusion(bf16[2048,2048]{1,0:T(8,128)(2,1)} %all-gather.10.cloned.1.call-done, f32[512,2048]{1,0:T(8,128)} %fusion.8), kind=kOutput, calls=%fused_computation.14 | convolution fusion | flops 4300210176 | bytes 16777216 | tf_op jit(solution)/shard_map/dot_general | solution.py:26
  277.7 0.0 reduce-scatter.4.cloned.1.call-update
  277.7 0.0 all-gather.14.cloned.1.call-start
  277.8 180.3 %reduce-scatter.8.cloned.1.call-done = f32[256,4096]{0,1:T(8,128)} async-done(((f32[2048,4096]{0,1:T(8,128)}), f32[256,4096]{0,1:T(8,128)}) %reduce-scatter.8.cloned.1.call-update) | async-done | bytes 4194320 | tf_op jit(solution)/shard_map/reduce_scatter | solution.py:54
  458.1 3.9 multiply_convert_fusion
  461.9 0.0 all-gather.14.cloned.1.call-update
  461.9 75.1 %reduce-scatter.6.cloned.1.call-done = f32[512,512]{1,0:T(8,128)} async-done(((f32[512,2048]{1,0:T(8,128)}), f32[512,512]{1,0:T(8,128)}) %reduce-scatter.6.cloned.1.call-update) | async-done | bytes 1048592 | tf_op jit(solution)/shard_map/reduce_scatter | solution.py:49
  537.1 2.1 convert_element_type.18
  539.2 77.5 %reduce-scatter.4.cloned.1.call-done = f32[512,512]{1,0:T(8,128)} async-done(((f32[512,2048]{1,0:T(8,128)}), f32[512,512]{1,0:T(8,128)}) %reduce-scatter.4.cloned.1.call-update) | async-done | bytes 1048592 | tf_op jit(solution)/shard_map/reduce_scatter | solution.py:45
  616.7 2.1 convert_element_type.16
  618.7 57.4 %all-gather.14.cloned.1.call-done = bf16[512,4096]{0,1:T(8,128)(2,1)} async-done(((bf16[256,4096]{0,1:T(8,128)(2,1)}), bf16[512,4096]{0,1:T(8,128)(2,1)}) %all-gather.14.cloned.1.call-update) | async-done | bytes 4194320 | tf_op jit(solution)/shard_map/all_gather | solution.py:61
  676.1 3.8 fusion.7
  679.9 2.4 copy.8
  (1 shorter events, 0.0 us)
Async XLA Ops:
  7.2 51.1 %all-gather.6.cloned.1.call-start = ((), (), s32[]{:S(2)}) async-start(), calls=%async_computation.3 | async-start | bytes 2621440 | tf_op jit(solution)/shard_map/all_gather | solution.py:35
  7.9 108.9 %all-gather.8.cloned.1.call-start = ((), (), s32[]{:S(2)}) async-start(), calls=%async_computation.4 | async-start | bytes 10485760 | tf_op jit(solution)/shard_map/all_gather | solution.py:39
  8.6 155.7 %all-gather.12.cloned.1.call-start = ((), (), s32[]{:S(2)}) async-start(), calls=%async_computation.7 | async-start | bytes 2621440 | tf_op jit(solution)/shard_map/all_gather | solution.py:36
  9.4 213.5 %all-gather.10.cloned.1.call-start = ((), (), s32[]{:S(2)}) async-start(), calls=%async_computation.5 | async-start | bytes 10485760 | tf_op jit(solution)/shard_map/all_gather | solution.py:40
  10.0 448.1 %reduce-scatter.8.cloned.1.call-start = ((), (), s32[]{:S(2)}) async-start(), calls=%async_computation.9 | async-start | bytes 37748736 | tf_op jit(solution)/shard_map/reduce_scatter | solution.py:54
  164.4 58.5 %copy-start = (bf16[512,2048]{1,0:T(8,128)(2,1)S(1)}, bf16[512,2048]{1,0:T(8,128)(2,1)}, u32[]{:S(2)}) copy-start(bf16[512,2048]{1,0:T(8,128)(2,1)} %all-gather.12.cloned.1.call-done) | copy-start | bytes 6291460
  222.8 17.9 %slice-start = ((s8[16777216]{0:T(1024)(128)(4,1)}), s8[4194304]{0:T(1024)(128)(4,1)S(1)}, s32[]{:S(2)}) async-start(s8[16777216]{0:T(1024)(128)(4,1)} %bitcast.16), calls=%async_computation.11 | async-start | bytes 8388608
  222.8 17.9 %slice-start.1 = ((s8[16777216]{0:T(1024)(128)(4,1)}), s8[4194304]{0:T(1024)(128)(4,1)S(1)}, s32[]{:S(2)}) async-start(s8[16777216]{0:T(1024)(128)(4,1)} %bitcast.16), calls=%async_computation.12 | async-start | bytes 8388608
  222.8 17.9 %slice-start.2 = ((s8[16777216]{0:T(1024)(128)(4,1)}), s8[4194304]{0:T(1024)(128)(4,1)S(1)}, s32[]{:S(2)}) async-start(s8[16777216]{0:T(1024)(128)(4,1)} %bitcast.16), calls=%async_computation.13 | async-start | bytes 8388608
  233.6 7.1 %slice-start.3 = ((s8[16777216]{0:T(1024)(128)(4,1)}), s8[4194304]{0:T(1024)(128)(4,1)S(1)}, s32[]{:S(2)}) async-start(s8[16777216]{0:T(1024)(128)(4,1)} %bitcast.16), calls=%async_computation.14 | async-start | bytes 8388608
  252.6 1.6 copy-start.1
  252.7 284.4 %reduce-scatter.6.cloned.1.call-start = ((), (), s32[]{:S(2)}) async-start(), calls=%async_computation.8 | async-start | bytes 5242880 | tf_op jit(solution)/shard_map/reduce_scatter | solution.py:49
  263.7 353.0 %reduce-scatter.4.cloned.1.call-start = ((), (), s32[]{:S(2)}) async-start(), calls=%async_computation.6 | async-start | bytes 5242880 | tf_op jit(solution)/shard_map/reduce_scatter | solution.py:45
  277.7 398.4 %all-gather.14.cloned.1.call-start = ((), (), s32[]{:S(2)}) async-start(), calls=%async_computation.10 | async-start | bytes 6291456 | tf_op jit(solution)/shard_map/all_gather | solution.py:61
Sparse Core Ops, SparseCore 0:
  9.6 48.6 all-gather.5
  59.8 56.9 all-gather.7
  118.4 45.9 all-gather.11
  165.8 57.0 all-gather.9
  252.8 205.2 reduce-scatter.7
  460.3 76.7 reduce-scatter.5
  539.4 77.2 reduce-scatter.3
  618.8 57.2 all-gather.13
where the time goes:
time: 689 us
  waiting for transfers between devices  580 us (84%)
  matrix products  66.7 us (10%)
  other arithmetic  19.9 us (3%)
  between operations  14.2 us (2%)
  local copies, waits for them, and re-layouts  7.71 us (1%)
    reduce_scatter x1, waiting for transfers between devices, local(): lax.psum_scatter(jnp.concatenate([contract_first(cot_all, act), contract_...  180 us
    reduce_scatter x1, waiting for transfers between devices, local(): lax.psum_scatter(out_term, 'col', scatter_dimension=1, tiled=True)  77.5 us
    reduce_scatter x1, waiting for transfers between devices, local(): lax.psum_scatter(back_term, 'col', scatter_dimension=1, tiled=True)  75.1 us
    all_gather x1, waiting for transfers between devices, local(): lax.all_gather(w_in, 'row', axis=1, tiled=True)  58.6 us
    all_gather x1, waiting for transfers between devices, local(): whole = lax.all_gather(finished, 'depth', axis=0, tiled=True)  57.4 us
    all_gather x1, waiting for transfers between devices, local(): lax.all_gather(tokens, 'col', axis=1, tiled=True)  48.2 us
    all_gather x1, waiting for transfers between devices, local(): lax.all_gather(w_out, 'row', axis=0, tiled=True)  43.3 us
    all_gather x1, waiting for transfers between devices, local(): lax.all_gather(grad_out, 'col', axis=1, tiled=True)  37 us
  transfers between devices with their start and end apart: 8, of which 8 were waited for; matrix products, arithmetic and copies ran while one was open for 8% of the time, Pallas kernels for 0%

commit v1 on v0

v1 whole, which is shorter than its diff:
```python
import functools
import math

import jax
import jax.numpy as jnp
from jax import lax
from jax.experimental import pallas as pl
from jax.experimental.pallas import tpu as pltpu
from jax.sharding import PartitionSpec as P

F32 = jnp.float32
BF16 = jnp.bfloat16
MESH = pl.DeviceIdType.MESH
ROWS = 32


def mm(left, right, ldim, rdim):
    return lax.dot_general(
        left, right, (((ldim,), (rdim,)), ((), ())), preferred_element_type=F32
    )


def wide(x):
    return x.astype(F32)


def kernel(
    nz, nd, fac,
    tok_in, win_in, wout_in, cot_in,
    out_ref, gtok_ref, gwin_ref, gwout_ref,
    tok, cot, win, wout, slope, act, dpre,
    psend, own, crecv, yrecv, xrecv, osend, orecv,
    loc_sem, zs, zr, as_, ar, cs, cr, ys, yr, xs, xr, os_, or_, fin_sem,
):
    T, D = tok.shape
    H = win.shape[0]
    bz, br = D // nz, D // 4
    hc = own.shape[3]
    nq = H // hc
    r = lax.axis_index("row")
    z = lax.axis_index("col")
    d = lax.axis_index("depth")
    c, y = lax.rem(r, 2), r // 2
    cp = y * 2 + (1 - c)
    yp = (1 - y) * 2 + c

    bar = pltpu.get_barrier_semaphore()
    for k in range(1, nz):
        pl.semaphore_signal(bar, inc=1, device_id={"col": lax.rem(z + k, nz)}, device_id_type=MESH)
    for k in range(1, nd):
        pl.semaphore_signal(bar, inc=1, device_id={"depth": lax.rem(d + k, nd)}, device_id_type=MESH)
    pl.semaphore_signal(bar, inc=1, device_id={"row": cp}, device_id_type=MESH)
    pl.semaphore_signal(bar, inc=1, device_id={"row": yp}, device_id_type=MESH)
    pl.semaphore_wait(bar, nz + nd)

    def send(src, dst, ss, rs, who):
        return pltpu.make_async_remote_copy(
            src_ref=src, dst_ref=dst, send_sem=ss, recv_sem=rs, device_id=who, device_id_type=MESH
        )

    def zcol(ref, i):
        return ref.at[:, pl.ds(pl.multiple_of(i * bz, bz), bz)]

    def wblk(a, i):
        at = pl.ds(pl.multiple_of(i * br, br), br)
        return win.at[:, at] if a == 0 else wout.at[at, :]

    acts_in, acts = (tok_in, cot_in), (tok, cot)
    w_in = (win_in, wout_in)

    def zcopy(a, k):
        return send(acts_in[a], zcol(acts[a], z), zs.at[a, k - 1], zr.at[a, k - 1], {"col": lax.rem(z + k, nz)})

    def ycopy(a):
        return send(w_in[a], wblk(a, r), as_.at[a, 0], ar.at[a, 0], {"row": yp})

    def ccopy(a):
        return send(w_in[a], wblk(a, r), as_.at[a, 1], ar.at[a, 1], {"row": cp})

    def fcopy(a):
        return send(wblk(a, yp), wblk(a, yp), as_.at[a, 2], ar.at[a, 2], {"row": cp})

    def lcopies(a):
        return (
            pltpu.make_async_copy(acts_in[a], zcol(acts[a], z), loc_sem.at[a, 0]),
            pltpu.make_async_copy(w_in[a], wblk(a, r), loc_sem.at[a, 1]),
        )

    for a in range(2):
        ycopy(a).start()
        for k in range(1, nz):
            zcopy(a, k).start()
        ccopy(a).start()
        for x in lcopies(a):
            x.start()

    def wait_acts(a):
        lcopies(a)[0].wait()
        for k in range(1, nz):
            zcopy(a, k).wait()

    def wait_weights(a):
        ycopy(a).wait()
        fcopy(a).start()
        lcopies(a)[1].wait()
        ccopy(a).wait()
        fcopy(a).wait()

    def hsl(q):
        return pl.ds(pl.multiple_of(q * hc, hc), hc)

    def rsl(i):
        return pl.ds(pl.multiple_of(i * ROWS, ROWS), ROWS)

    wait_acts(0)
    wait_weights(0)

    @pl.loop(0, nq)
    def _(q):
        slope[:, hsl(q)] = mm(tok[...], win[hsl(q), :], 1, 1)

        @pl.loop(0, T // ROWS)
        def _(i):
            v = slope[rsl(i), hsl(q)]
            half = 0.5 * (1.0 + lax.erf(v * (1.0 / math.sqrt(2.0))))
            act[rsl(i), hsl(q)] = (v * half).astype(BF16)
            slope[rsl(i), hsl(q)] = half + v * jnp.exp(-0.5 * v * v) * (1.0 / math.sqrt(2.0 * math.pi))

    def core_copy(u, slot):
        return send(psend.at[slot], crecv.at[u], cs.at[slot], cr.at[u], {"row": cp})

    def y_copy(u):
        return send(own.at[u, 1 - y], yrecv.at[u], ys.at[u], yr.at[u], {"row": yp})

    def ufinal(u):
        return own.at[u, y] if nd == 2 else xrecv.at[u, d]

    def x_copy(u, k):
        dst = xrecv.at[u, 0] if nd == 2 else xrecv.at[u, d]
        return send(ufinal(u), dst, xs.at[u, k - 1], xr.at[u, k - 1], {"depth": lax.rem(d + k, nd)})

    def fold(u):
        core_copy(u, lax.rem(u, 2)).wait_recv()

        @pl.loop(0, hc // ROWS)
        def _(i):
            own[u, 1 - y, rsl(i), :] = (
                wide(own[u, 1 - y, rsl(i), :]) + wide(crecv[u, 1 - y, rsl(i), :])
            ).astype(BF16)

        y_copy(u).start()

    def fold_rows(u):
        y_copy(u).wait_recv()
        dst = ufinal(u)

        @pl.loop(0, hc // ROWS)
        def _(i):
            dst[rsl(i), :] = (
                wide(own[u, y, rsl(i), :]) + wide(crecv[u, y, rsl(i), :]) + wide(yrecv[u, rsl(i), :])
            ).astype(BF16)

        for k in range(1, nd):
            x_copy(u, k).start()

    def final_copy(a, q):
        u = a * nq + q
        dst = gwout_ref.at[:, hsl(q)] if a == 0 else gwin_ref.at[hsl(q), :]
        return pltpu.make_async_copy(yrecv.at[u], dst, fin_sem.at[u])

    def finish(a, q):
        u = a * nq + q
        for k in range(1, nd):
            x_copy(u, k).wait_recv()

        @pl.loop(0, hc // ROWS)
        def _(i):
            if nd == 2:
                total = wide(own[u, y, rsl(i), :]) + wide(xrecv[u, 0, rsl(i), :])
            else:
                total = wide(xrecv[u, 0, rsl(i), :])
                for e in range(1, nd):
                    total = total + wide(xrecv[u, e, rsl(i), :])
            yrecv[u, rsl(i), :] = (total * fac).astype(BF16)

        final_copy(a, q).start()

    def produce(a):
        left_all = cot if a == 0 else tok

        @pl.loop(0, nq)
        def _(q):
            u = a * nq + q
            slot = lax.rem(u, 2)

            @pl.when(u >= 2)
            def _():
                core_copy(u, slot).wait_send()

            for mine in range(2):
                for yy in range(2):
                    owner = yy * 2 + (c if mine else 1 - c)
                    feats = left_all[:, pl.ds(pl.multiple_of(owner * br, br), br)]
                    if a == 0:
                        tile = mm(feats, act[:, hsl(q)], 0, 0)
                    else:
                        tile = mm(dpre[:, hsl(q)], feats, 0, 0)
                    if mine:
                        own[u, yy] = tile.astype(BF16)
                    else:
                        psend[slot, yy] = tile.astype(BF16)
                if not mine:
                    core_copy(u, slot).start()

            @pl.when(u >= 1)
            def _():
                fold(u - 1)

    def out_copy(a, k):
        return send(osend.at[a, k - 1], orecv.at[a, k - 1], os_.at[a, k - 1], or_.at[a, k - 1], {"col": lax.rem(z + k, nz)})

    def terms(a):
        for k in range(1, nz + 1):
            to = lax.rem(z + k, nz)
            at = pl.ds(pl.multiple_of(to * bz, bz), bz)
            term = mm(act[...], wout[at, :], 1, 1) if a == 0 else mm(dpre[...], win[:, at], 1, 0)
            if k < nz:
                osend[a, k - 1] = term.astype(BF16)
                out_copy(a, k).start()
            else:
                slope[:, a * bz : (a + 1) * bz] = term

    wait_acts(1)
    produce(0)
    wait_weights(1)

    @pl.loop(0, nq)
    def _(q):
        slope[:, hsl(q)] = slope[:, hsl(q)] * mm(cot[...], wout[:, hsl(q)], 1, 0)
        dpre[:, hsl(q)] = slope[:, hsl(q)].astype(BF16)

    produce(1)
    fold(2 * nq - 1)
    terms(0)
    terms(1)

    total_units = 2 * nq

    def drain(a):
        @pl.loop(0, nq)
        def _(q):
            u = a * nq + q
            fold_rows(u)
            if a == 1:
                finish(0, q)

    drain(0)
    drain(1)

    def out_final(a):
        return pltpu.make_async_copy(orecv.at[a, 0], (out_ref, gtok_ref)[a], fin_sem.at[total_units + a])

    for a in range(2):
        for k in range(1, nz):
            out_copy(a, k).wait()

        @pl.loop(0, T // ROWS)
        def _(i):
            total = slope[rsl(i), a * bz : (a + 1) * bz]
            for k in range(1, nz):
                total = total + wide(orecv[a, k - 1, rsl(i), :])
            orecv[a, 0, rsl(i), :] = total.astype(BF16)

        out_final(a).start()

    @pl.loop(0, nq)
    def _(q):
        finish(1, q)

    for s in range(2):
        core_copy(total_units - 2 + s, (total_units - 2 + s) % 2).wait_send()

    for a in range(2):
        out_final(a).wait()

        @pl.loop(0, nq)
        def _(q):
            u = a * nq + q
            y_copy(u).wait_send()
            for k in range(1, nd):
                x_copy(u, k).wait_send()
            final_copy(a, q).wait()


def local(nz, nd, tokens, w_in, w_out, grad_out):
    T, bz = tokens.shape
    D = bz * nz
    H = w_in.shape[0]
    br = w_in.shape[1]
    hc = br
    nq = H // hc
    nx = 1 if nd == 2 else nd
    fac = 1.0 / math.sqrt(T * 4 * nd)
    dma = pltpu.SemaphoreType.DMA
    anyspec = pl.BlockSpec(memory_space=pl.ANY)
    flops = 12 * T * D * H
    return pl.pallas_call(
        functools.partial(kernel, nz, nd, fac),
        out_shape=(
            jax.ShapeDtypeStruct((T, bz), BF16),
            jax.ShapeDtypeStruct((T, bz), BF16),
            jax.ShapeDtypeStruct((H, br), BF16),
            jax.ShapeDtypeStruct((br, H), BF16),
        ),
        in_specs=[anyspec] * 4,
        out_specs=(anyspec,) * 4,
        scratch_shapes=[
            pltpu.VMEM((T, D), BF16),
            pltpu.VMEM((T, D), BF16),
            pltpu.VMEM((H, D), BF16),
            pltpu.VMEM((D, H), BF16),
            pltpu.VMEM((T, H), F32),
            pltpu.VMEM((T, H), BF16),
            pltpu.VMEM((T, H), BF16),
            pltpu.VMEM((2, 2, hc, br), BF16),
            pltpu.VMEM((2 * nq, 2, hc, br), BF16),
            pltpu.VMEM((2 * nq, 2, hc, br), BF16),
            pltpu.VMEM((2 * nq, hc, br), BF16),
            pltpu.VMEM((2 * nq, nx, hc, br), BF16),
            pltpu.VMEM((2, nz - 1, T, bz), BF16),
            pltpu.VMEM((2, nz - 1, T, bz), BF16),
            dma((2, 2)),
            dma((2, nz - 1)),
            dma((2, nz - 1)),
            dma((2, 3)),
            dma((2, 3)),
            dma((2,)),
            dma((2 * nq,)),
            dma((2 * nq,)),
            dma((2 * nq,)),
            dma((2 * nq, max(nd - 1, 1))),
            dma((2 * nq, max(nd - 1, 1))),
            dma((2, nz - 1)),
            dma((2, nz - 1)),
            dma((2 * nq + 2,)),
        ],
        compiler_params=pltpu.CompilerParams(
            collective_id=0, has_side_effects=True, vmem_limit_bytes=VMEM_LIMIT
        ),
        cost_estimate=pl.CostEstimate(flops=flops, bytes_accessed=20 * 2**20, transcendentals=2 * T * H),
        name="mlp",
    )(tokens, w_in, w_out, grad_out)


VMEM_LIMIT = 64 * 2**20 - 2**16


def solution(mesh):
    nz, nd = mesh.shape["col"], mesh.shape["depth"]
    in_specs = (
        P(("depth", "row"), "col"),
        P("col", "row"),
        P("row", "col"),
        P(("depth", "row"), "col"),
    )
    out_specs = (
        P(("depth", "row"), "col"),
        P(("depth", "row"), "col"),
        P("col", "row"),
        P("row", "col"),
    )
    return jax.shard_map(
        functools.partial(local, nz, nd), mesh=mesh, in_specs=in_specs, out_specs=out_specs, check_vma=False
    )
```

time: 689 us -> 232 us (0.34)
  waiting for transfers between devices: 580 us -> 0 us
  Pallas kernels: 0 us -> 220 us
  matrix products: 66.7 us -> 0 us
  other arithmetic: 19.9 us -> 0 us
  between operations: 14.2 us -> 0.65 us
    reduce_scatter x3 -> x0, waiting for transfers between devices: 333 us -> none  [the longest x1 180 us: local(): lax.psum_scatter(jnp.concatenate([contract_first(cot_all, act), contract_...]
    all_gather x5 -> x0, waiting for transfers between devices: 245 us -> none  [the longest x1 58.6 us: local(): lax.all_gather(w_in, 'row', axis=1, tiled=True)]
    pallas_call x0 -> x1, Pallas kernels: none -> 220 us  [local(): pl.pallas_call(functools.partial(kernel, nz, nd, fac), out_shape=(jax.Sha...]
    dot_general x6 -> x0, matrix products: 66.7 us -> none  [the longest x2 24.3 us: contract_last(): lax.dot_general(left, right, (((1,), (1,)), ((), ())), preferred_element_...]
    concatenate x1 -> x0, other arithmetic: 11.9 us -> none  [local(): jnp.concatenate([contract_first(cot_all, act), contract_first(tok_all, d_...]
    convert_element_type x3 -> x0, other arithmetic: 8.04 us -> none  [the longest x1 3.87 us: local(): finished = (summed * factor).astype(jnp.bfloat16)]
  transfers between devices with their start and end apart: 8 -> 0, of which waited for: 8 -> 0; matrix products, arithmetic and copies ran while one was open for 8% -> 0% of each run, Pallas kernels for 0% -> 0%
where the time goes in v1:
time: 232 us; the launch traced here: 229 us
  Pallas kernels  220 us (95%)
  local copies, waits for them, and re-layouts  7.55 us (3%)
    pallas_call x1, Pallas kernels, local(): pl.pallas_call(functools.partial(kernel, nz, nd, fac), out_shape=(jax.Sha...  220 us
    unnamed x8, local copies, waits for them, and re-layouts  7.55 us

profile of v1, /device:TPU:0, one launch (start us, length us, event | category | flops | bytes accessed | tf_op | source)
XLA Modules:
  0.0 228.7 jit_solution(3619255285301016594)
XLA Ops:
  0.6 220.5 %mlp.1 = (bf16[512,512]{1,0:T(8,128)(2,1)}, bf16[512,512]{1,0:T(8,128)(2,1)}, bf16[2048,512]{1,0:T(8,128)(2,1)}, bf16[512,2048]{1,0:T(8,128)(2,1)}) custom-call(bf16[512,512]{1,0:T(8,128)(2,1)} %tok_in.1, bf16[2048,512]{1,0:T(8,128)(2,1)} %win_in.1, bf16[512,2048]{1,0:T(8,128)(2,1)} %wout_in.1, bf16[512,512]{1,0:T(8,128)(2,1)} %cot_in.1), custom_call_target="tpu_custom_call" | custom-call | flops 25769803776 | bytes 20971520 | tf_op jit(solution)/shard_map/mlp/pallas_call | solution.py:307
  221.1 0.0 copy-start.1
  221.1 2.0 copy.12
  223.1 1.9 copy.13
  225.0 0.0 copy-done.1
  225.0 0.0 copy-start
  225.0 1.3 copy.14
  226.3 1.0 copy-done
  227.4 1.3 copy.15
Async XLA Ops:
  221.1 3.9 %copy-start.1 = (bf16[2048,512]{1,0:T(8,128)(2,1)S(1)}, bf16[2048,512]{1,0:T(8,128)(2,1)}, u32[]{:S(2)}) copy-start(bf16[2048,512]{1,0:T(8,128)(2,1)} %get-tuple-element.10) | copy-start | bytes 6291460
  225.0 2.3 %copy-start = (bf16[512,2048]{1,0:T(8,128)(2,1)S(1)}, bf16[512,2048]{1,0:T(8,128)(2,1)}, u32[]{:S(2)}) copy-start(bf16[512,2048]{1,0:T(8,128)(2,1)} %get-tuple-element.11) | copy-start | bytes 6291460

commit v2 on v1

--- a/solution.py
+++ b/solution.py
@@ -29,7 +29,7 @@
     tok_in, win_in, wout_in, cot_in,
     out_ref, gtok_ref, gwin_ref, gwout_ref,
     tok, cot, win, wout, slope, act, dpre,
-    psend, own, crecv, yrecv, xrecv, osend, orecv,
+    psend, own, crecv, yrecv, xrecv, osend, orecv, mine_f32,
     loc_sem, zs, zr, as_, ar, cs, cr, ys, yr, xs, xr, os_, or_, fin_sem,
 ):
     T, D = tok.shape
@@ -68,17 +68,57 @@
     acts_in, acts = (tok_in, cot_in), (tok, cot)
     w_in = (win_in, wout_in)
 
-    def zcopy(a, k):
-        return send(acts_in[a], zcol(acts[a], z), zs.at[a, k - 1], zr.at[a, k - 1], {"col": lax.rem(z + k, nz)})
+    def zhop(a, way, s):
+        shard = z - s if way == 0 else z + s
+        to = lax.rem(z + (1 if way == 0 else nz - 1), nz)
+        src = acts_in[a] if s == 0 else zcol(acts[a], shard)
+        return send(src, zcol(acts[a], shard), zs.at[a, way, s], zr.at[a, way, s], {"col": to})
+
+    def sends(way, s):
+        if way == 0:
+            return jnp.logical_and(z >= s, z < nz - 1)
+        return jnp.logical_and(z < nz - s, z > 0)
+
+    def gets(way, s):
+        return z >= s + 1 if way == 0 else z < nz - 1 - s
+
+    def zstart(a, s):
+        for way in range(2):
+            pl.when(sends(way, s))(lambda way=way: zhop(a, way, s).start())
+
+    def zwait(a, s):
+        for way in range(2):
+            pl.when(gets(way, s))(lambda way=way: zhop(a, way, s).wait_recv())
+
+    def zdone(a):
+        for s in range(nz - 1):
+            for way in range(2):
+                pl.when(sends(way, s))(lambda way=way, s=s: zhop(a, way, s).wait_send())
+
+    def part(a, shard, e):
+        if a == 0:
+            n = H // nd
+            return win.at[
+                pl.ds(pl.multiple_of(e * n, n), n), pl.ds(pl.multiple_of(shard * br, br), br)
+            ]
+        n = br // nd
+        return wout.at[pl.ds(pl.multiple_of(shard * br + e * n, n), n), :]
 
     def ycopy(a):
-        return send(w_in[a], wblk(a, r), as_.at[a, 0], ar.at[a, 0], {"row": yp})
+        n = (H if a == 0 else br) // nd
+        src = w_in[a].at[pl.ds(pl.multiple_of(d * n, n), n), :]
+        return send(src, part(a, r, d), as_.at[a, 0], ar.at[a, 0], {"row": yp})
 
     def ccopy(a):
         return send(w_in[a], wblk(a, r), as_.at[a, 1], ar.at[a, 1], {"row": cp})
 
-    def fcopy(a):
-        return send(wblk(a, yp), wblk(a, yp), as_.at[a, 2], ar.at[a, 2], {"row": cp})
+    def dcopy(a, k):
+        p = part(a, yp, d)
+        return send(p, p, as_.at[a, 1 + k], ar.at[a, 1 + k], {"depth": lax.rem(d + k, nd)})
+
+    def fcopy(a, k):
+        p = part(a, yp, lax.rem(d + nd - k, nd))
+        return send(p, p, as_.at[a, 1 + nd + k], ar.at[a, 1 + nd + k], {"row": cp})
 
     def lcopies(a):
         return (
@@ -86,25 +126,50 @@
             pltpu.make_async_copy(w_in[a], wblk(a, r), loc_sem.at[a, 1]),
         )
 
+    def weights_hop(a):
+        ycopy(a).wait_recv()
+        for k in range(1, nd):
+            dcopy(a, k).start()
+        fcopy(a, 0).start()
+
+    def weights_end(a):
+        for k in range(1, nd):
+            dcopy(a, k).wait_recv()
+            fcopy(a, k).start()
+        lcopies(a)[1].wait()
+        ccopy(a).wait()
+        ycopy(a).wait_send()
+        for k in range(1, nd):
+            dcopy(a, k).wait_send()
+        for k in range(nd):
+            fcopy(a, k).wait()
+
+    ycopy(0).start()
+    zstart(0, 0)
     for a in range(2):
-        ycopy(a).start()
-        for k in range(1, nz):
-            zcopy(a, k).start()
         ccopy(a).start()
         for x in lcopies(a):
             x.start()
-
-    def wait_acts(a):
-        lcopies(a)[0].wait()
-        for k in range(1, nz):
-            zcopy(a, k).wait()
-
-    def wait_weights(a):
-        ycopy(a).wait()
-        fcopy(a).start()
-        lcopies(a)[1].wait()
-        ccopy(a).wait()
-        fcopy(a).wait()
+    zwait(0, 0)
+    if nz > 2:
+        zstart(0, 1)
+    weights_hop(0)
+    ycopy(1).start()
+    for s in range(2, nz - 1):
+        zwait(0, s - 1)
+        zstart(0, s)
+    zstart(1, 0)
+    if nz > 2:
+        zwait(0, nz - 2)
+    lcopies(0)[0].wait()
+    weights_end(0)
+
+    def cot_hop(s):
+        zwait(1, s - 1)
+        zstart(1, s)
+
+    hooks = [functools.partial(cot_hop, s) for s in range(1, nz - 1)]
+    hooks.insert(1, functools.partial(weights_hop, 1))
 
     def hsl(q):
         return pl.ds(pl.multiple_of(q * hc, hc), hc)
@@ -112,11 +177,10 @@
     def rsl(i):
         return pl.ds(pl.multiple_of(i * ROWS, ROWS), ROWS)
 
-    wait_acts(0)
-    wait_weights(0)
-
     @pl.loop(0, nq)
     def _(q):
+        for i, hook in enumerate(hooks[:nq]):
+            pl.when(q == i)(hook)
         slope[:, hsl(q)] = mm(tok[...], win[hsl(q), :], 1, 1)
 
         @pl.loop(0, T // ROWS)
@@ -216,6 +280,9 @@
             def _():
                 fold(u - 1)
 
+            if a == 1:
+                fold_rows(q)
+
     def out_copy(a, k):
         return send(osend.at[a, k - 1], orecv.at[a, k - 1], os_.at[a, k - 1], or_.at[a, k - 1], {"col": lax.rem(z + k, nz)})
 
@@ -228,34 +295,35 @@
                 osend[a, k - 1] = term.astype(BF16)
                 out_copy(a, k).start()
             else:
-                slope[:, a * bz : (a + 1) * bz] = term
-
-    wait_acts(1)
+                mine_f32[a] = term
+
+    for hook in hooks[nq:]:
+        hook()
+    zwait(1, nz - 2)
+    lcopies(1)[0].wait()
+
     produce(0)
-    wait_weights(1)
+    weights_end(1)
+    terms(0)
 
     @pl.loop(0, nq)
     def _(q):
         slope[:, hsl(q)] = slope[:, hsl(q)] * mm(cot[...], wout[:, hsl(q)], 1, 0)
         dpre[:, hsl(q)] = slope[:, hsl(q)].astype(BF16)
 
+    terms(1)
     produce(1)
     fold(2 * nq - 1)
-    terms(0)
-    terms(1)
 
     total_units = 2 * nq
 
-    def drain(a):
+    def drain():
         @pl.loop(0, nq)
         def _(q):
-            u = a * nq + q
-            fold_rows(u)
-            if a == 1:
-                finish(0, q)
-
-    drain(0)
-    drain(1)
+            fold_rows(nq + q)
+            finish(0, q)
+
+    drain()
 
     def out_final(a):
         return pltpu.make_async_copy(orecv.at[a, 0], (out_ref, gtok_ref)[a], fin_sem.at[total_units + a])
@@ -266,7 +334,7 @@
 
         @pl.loop(0, T // ROWS)
         def _(i):
-            total = slope[rsl(i), a * bz : (a + 1) * bz]
+            total = mine_f32[a, rsl(i), :]
             for k in range(1, nz):
                 total = total + wide(orecv[a, k - 1, rsl(i), :])
             orecv[a, 0, rsl(i), :] = total.astype(BF16)
@@ -281,6 +349,7 @@
         core_copy(total_units - 2 + s, (total_units - 2 + s) % 2).wait_send()
 
     for a in range(2):
+        zdone(a)
         out_final(a).wait()
 
         @pl.loop(0, nq)
@@ -329,11 +398,12 @@
             pltpu.VMEM((2 * nq, nx, hc, br), BF16),
             pltpu.VMEM((2, nz - 1, T, bz), BF16),
             pltpu.VMEM((2, nz - 1, T, bz), BF16),
+            pltpu.VMEM((2, T, bz), F32),
             dma((2, 2)),
-            dma((2, nz - 1)),
-            dma((2, nz - 1)),
-            dma((2, 3)),
-            dma((2, 3)),
+            dma((2, 2, nz - 1)),
+            dma((2, 2, nz - 1)),
+            dma((2, 1 + 2 * nd)),
+            dma((2, 1 + 2 * nd)),
             dma((2,)),
             dma((2 * nq,)),
             dma((2 * nq,)),

time: 232 us -> 210 us (0.905); the launches traced: 229 us -> 210 us
  Pallas kernels: 220 us -> 202 us
    pallas_call x1, Pallas kernels: 220 us -> 202 us  [local(): pl.pallas_call(functools.partial(kernel, nz, nd, fac), out_shape=(jax.Sha...]
where the time goes in v2:
time: 210 us
  Pallas kernels  202 us (96%)
  local copies, waits for them, and re-layouts  7.55 us (4%)
    pallas_call x1, Pallas kernels, local(): pl.pallas_call(functools.partial(kernel, nz, nd, fac), out_shape=(jax.Sha...  202 us
    unnamed x8, local copies, waits for them, and re-layouts  7.55 us

profile of v2, /device:TPU:0, one launch (start us, length us, event | category | flops | bytes accessed | tf_op | source)
XLA Modules:
  0.0 210.0 jit_solution(5871958120833002130)
XLA Ops:
  0.6 201.8 %mlp.1 = (bf16[512,512]{1,0:T(8,128)(2,1)}, bf16[512,512]{1,0:T(8,128)(2,1)}, bf16[2048,512]{1,0:T(8,128)(2,1)}, bf16[512,2048]{1,0:T(8,128)(2,1)}) custom-call(bf16[512,512]{1,0:T(8,128)(2,1)} %tok_in.1, bf16[2048,512]{1,0:T(8,128)(2,1)} %win_in.1, bf16[512,2048]{1,0:T(8,128)(2,1)} %wout_in.1, bf16[512,512]{1,0:T(8,128)(2,1)} %cot_in.1), custom_call_target="tpu_custom_call" | custom-call | flops 25769803776 | bytes 20971520 | tf_op jit(solution)/shard_map/mlp/pallas_call | solution.py:376
  202.5 0.0 copy-start.1
  202.5 2.0 copy.12
  204.5 1.9 copy.13
  206.4 0.0 copy-done.1
  206.4 0.0 copy-start
  206.4 1.3 copy.14
  207.7 1.0 copy-done
  208.7 1.3 copy.15
Async XLA Ops:
  202.5 3.9 %copy-start.1 = (bf16[2048,512]{1,0:T(8,128)(2,1)S(1)}, bf16[2048,512]{1,0:T(8,128)(2,1)}, u32[]{:S(2)}) copy-start(bf16[2048,512]{1,0:T(8,128)(2,1)} %get-tuple-element.10) | copy-start | bytes 6291460
  206.4 2.3 %copy-start = (bf16[512,2048]{1,0:T(8,128)(2,1)S(1)}, bf16[512,2048]{1,0:T(8,128)(2,1)}, u32[]{:S(2)}) copy-start(bf16[512,2048]{1,0:T(8,128)(2,1)} %get-tuple-element.11) | copy-start | bytes 6291460

commit v3 on v2

--- a/solution.py
+++ b/solution.py
@@ -35,8 +35,9 @@
     T, D = tok.shape
     H = win.shape[0]
     bz, br = D // nz, D // 4
-    hc = own.shape[3]
-    nq = H // hc
+    hr, hc = own.shape[2:]
+    nq, ns = H // hc, hc // hr
+    nu = nq * ns
     r = lax.axis_index("row")
     z = lax.axis_index("col")
     d = lax.axis_index("depth")
@@ -206,7 +207,7 @@
     def fold(u):
         core_copy(u, lax.rem(u, 2)).wait_recv()
 
-        @pl.loop(0, hc // ROWS)
+        @pl.loop(0, hr // ROWS)
         def _(i):
             own[u, 1 - y, rsl(i), :] = (
                 wide(own[u, 1 - y, rsl(i), :]) + wide(crecv[u, 1 - y, rsl(i), :])
@@ -218,7 +219,7 @@
         y_copy(u).wait_recv()
         dst = ufinal(u)
 
-        @pl.loop(0, hc // ROWS)
+        @pl.loop(0, hr // ROWS)
         def _(i):
             dst[rsl(i), :] = (
                 wide(own[u, y, rsl(i), :]) + wide(crecv[u, y, rsl(i), :]) + wide(yrecv[u, rsl(i), :])
@@ -227,17 +228,23 @@
         for k in range(1, nd):
             x_copy(u, k).start()
 
-    def final_copy(a, q):
-        u = a * nq + q
-        dst = gwout_ref.at[:, hsl(q)] if a == 0 else gwin_ref.at[hsl(q), :]
+    def rows_at(w):
+        return pl.ds(pl.multiple_of(w * hr, hr), hr)
+
+    def final_copy(a, w):
+        u = a * nu + w
+        if a == 0:
+            dst = gwout_ref.at[rows_at(lax.rem(w, ns)), hsl(w // ns)]
+        else:
+            dst = gwin_ref.at[rows_at(w), :]
         return pltpu.make_async_copy(yrecv.at[u], dst, fin_sem.at[u])
 
-    def finish(a, q):
-        u = a * nq + q
+    def finish(a, w):
+        u = a * nu + w
         for k in range(1, nd):
             x_copy(u, k).wait_recv()
 
-        @pl.loop(0, hc // ROWS)
+        @pl.loop(0, hr // ROWS)
         def _(i):
             if nd == 2:
                 total = wide(own[u, y, rsl(i), :]) + wide(xrecv[u, 0, rsl(i), :])
@@ -247,14 +254,12 @@
                     total = total + wide(xrecv[u, e, rsl(i), :])
             yrecv[u, rsl(i), :] = (total * fac).astype(BF16)
 
-        final_copy(a, q).start()
+        final_copy(a, w).start()
 
     def produce(a):
-        left_all = cot if a == 0 else tok
-
-        @pl.loop(0, nq)
-        def _(q):
-            u = a * nq + q
+        @pl.loop(0, nu)
+        def _(w):
+            u = a * nu + w
             slot = lax.rem(u, 2)
 
             @pl.when(u >= 2)
@@ -264,11 +269,13 @@
             for mine in range(2):
                 for yy in range(2):
                     owner = yy * 2 + (c if mine else 1 - c)
-                    feats = left_all[:, pl.ds(pl.multiple_of(owner * br, br), br)]
                     if a == 0:
-                        tile = mm(feats, act[:, hsl(q)], 0, 0)
+                        base = owner * br + lax.rem(w, ns) * hr
+                        feats = cot[:, pl.ds(pl.multiple_of(base, hr), hr)]
+                        tile = mm(feats, act[:, hsl(w // ns)], 0, 0)
                     else:
-                        tile = mm(dpre[:, hsl(q)], feats, 0, 0)
+                        feats = tok[:, pl.ds(pl.multiple_of(owner * br, br), br)]
+                        tile = mm(dpre[:, rows_at(w)], feats, 0, 0)
                     if mine:
                         own[u, yy] = tile.astype(BF16)
                     else:
@@ -276,12 +283,15 @@
                 if not mine:
                     core_copy(u, slot).start()
 
-            @pl.when(u >= 1)
+            @pl.when(w >= 1)
             def _():
                 fold(u - 1)
 
             if a == 1:
-                fold_rows(q)
+                for i, j in enumerate(range(cuts[3], nu)):
+                    pl.when(w == min(1 + 4 * i, nu - 1))(functools.partial(fold_rows, j))
+
+        fold(a * nu + nu - 1)
 
     def out_copy(a, k):
         return send(osend.at[a, k - 1], orecv.at[a, k - 1], os_.at[a, k - 1], or_.at[a, k - 1], {"col": lax.rem(z + k, nz)})
@@ -302,26 +312,34 @@
     zwait(1, nz - 2)
     lcopies(1)[0].wait()
 
+    cuts = (nu // 4, 3 * nu // 8, 5 * nu // 8, 6 * nu // 8)
     produce(0)
+    for j in range(cuts[0]):
+        fold_rows(j)
     weights_end(1)
     terms(0)
+    for j in range(cuts[0], cuts[1]):
+        fold_rows(j)
 
     @pl.loop(0, nq)
     def _(q):
         slope[:, hsl(q)] = slope[:, hsl(q)] * mm(cot[...], wout[:, hsl(q)], 1, 0)
         dpre[:, hsl(q)] = slope[:, hsl(q)].astype(BF16)
 
+    for j in range(cuts[1], cuts[2]):
+        fold_rows(j)
     terms(1)
+    for j in range(cuts[2], cuts[3]):
+        fold_rows(j)
     produce(1)
-    fold(2 * nq - 1)
-
-    total_units = 2 * nq
+
+    total_units = 2 * nu
 
     def drain():
-        @pl.loop(0, nq)
-        def _(q):
-            fold_rows(nq + q)
-            finish(0, q)
+        @pl.loop(0, nu)
+        def _(w):
+            fold_rows(nu + w)
+            finish(0, w)
 
     drain()
 
@@ -341,9 +359,9 @@
 
         out_final(a).start()
 
-    @pl.loop(0, nq)
-    def _(q):
-        finish(1, q)
+    @pl.loop(0, nu)
+    def _(w):
+        finish(1, w)
 
     for s in range(2):
         core_copy(total_units - 2 + s, (total_units - 2 + s) % 2).wait_send()
@@ -352,13 +370,13 @@
         zdone(a)
         out_final(a).wait()
 
-        @pl.loop(0, nq)
-        def _(q):
-            u = a * nq + q
+        @pl.loop(0, nu)
+        def _(w):
+            u = a * nu + w
             y_copy(u).wait_send()
             for k in range(1, nd):
                 x_copy(u, k).wait_send()
-            final_copy(a, q).wait()
+            final_copy(a, w).wait()
 
 
 def local(nz, nd, tokens, w_in, w_out, grad_out):
@@ -367,7 +385,8 @@
     H = w_in.shape[0]
     br = w_in.shape[1]
     hc = br
-    nq = H // hc
+    hr = hc // 2
+    nu = 2 * (H // hc)
     nx = 1 if nd == 2 else nd
     fac = 1.0 / math.sqrt(T * 4 * nd)
     dma = pltpu.SemaphoreType.DMA
@@ -391,11 +410,11 @@
             pltpu.VMEM((T, H), F32),
             pltpu.VMEM((T, H), BF16),
             pltpu.VMEM((T, H), BF16),
-            pltpu.VMEM((2, 2, hc, br), BF16),
-            pltpu.VMEM((2 * nq, 2, hc, br), BF16),
-            pltpu.VMEM((2 * nq, 2, hc, br), BF16),
-            pltpu.VMEM((2 * nq, hc, br), BF16),
-            pltpu.VMEM((2 * nq, nx, hc, br), BF16),
+            pltpu.VMEM((2, 2, hr, br), BF16),
+            pltpu.VMEM((2 * nu, 2, hr, br), BF16),
+            pltpu.VMEM((2 * nu, 2, hr, br), BF16),
+            pltpu.VMEM((2 * nu, hr, br), BF16),
+            pltpu.VMEM((2 * nu, nx, hr, br), BF16),
             pltpu.VMEM((2, nz - 1, T, bz), BF16),
             pltpu.VMEM((2, nz - 1, T, bz), BF16),
             pltpu.VMEM((2, T, bz), F32),
@@ -405,14 +424,14 @@
             dma((2, 1 + 2 * nd)),
             dma((2, 1 + 2 * nd)),
             dma((2,)),
-            dma((2 * nq,)),
-            dma((2 * nq,)),
-            dma((2 * nq,)),
-            dma((2 * nq, max(nd - 1, 1))),
-            dma((2 * nq, max(nd - 1, 1))),
+            dma((2 * nu,)),
+            dma((2 * nu,)),
+            dma((2 * nu,)),
+            dma((2 * nu, max(nd - 1, 1))),
+            dma((2 * nu, max(nd - 1, 1))),
             dma((2, nz - 1)),
             dma((2, nz - 1)),
-            dma((2 * nq + 2,)),
+            dma((2 * nu + 2,)),
         ],
         compiler_params=pltpu.CompilerParams(
             collective_id=0, has_side_effects=True, vmem_limit_bytes=VMEM_LIMIT

time: 210 us -> 195 us (0.929)
  Pallas kernels: 202 us -> 187 us
    pallas_call x1, Pallas kernels: 202 us -> 187 us  [local(): pl.pallas_call(functools.partial(kernel, nz, nd, fac), out_shape=(jax.Sha...]
where the time goes in v3:
time: 195 us
  Pallas kernels  187 us (96%)
  local copies, waits for them, and re-layouts  7.55 us (4%)
    pallas_call x1, Pallas kernels, local(): pl.pallas_call(functools.partial(kernel, nz, nd, fac), out_shape=(jax.Sha...  187 us
    unnamed x8, local copies, waits for them, and re-layouts  7.55 us

profile of v3, /device:TPU:0, one launch (start us, length us, event | category | flops | bytes accessed | tf_op | source)
XLA Modules:
  0.0 195.1 jit_solution(2677518071614791902)
XLA Ops:
  0.6 186.9 %mlp.1 = (bf16[512,512]{1,0:T(8,128)(2,1)}, bf16[512,512]{1,0:T(8,128)(2,1)}, bf16[2048,512]{1,0:T(8,128)(2,1)}, bf16[512,2048]{1,0:T(8,128)(2,1)}) custom-call(bf16[512,512]{1,0:T(8,128)(2,1)} %tok_in.1, bf16[2048,512]{1,0:T(8,128)(2,1)} %win_in.1, bf16[512,2048]{1,0:T(8,128)(2,1)} %wout_in.1, bf16[512,512]{1,0:T(8,128)(2,1)} %cot_in.1), custom_call_target="tpu_custom_call" | custom-call | flops 25769803776 | bytes 20971520 | tf_op jit(solution)/shard_map/mlp/pallas_call | solution.py:395
  187.6 0.0 copy-start.1
  187.6 2.0 %copy.12 = bf16[512,512]{1,0:T(8,128)(2,1)} copy(bf16[512,512]{1,0:T(8,128)(2,1)} %get-tuple-element.8) | data formatting | bytes 1048576
  189.6 1.9 copy.13
  191.5 0.0 copy-done.1
  191.5 0.0 copy-start
  191.5 1.3 copy.14
  192.8 1.0 copy-done
  193.8 1.3 copy.15
Async XLA Ops:
  187.6 3.9 %copy-start.1 = (bf16[2048,512]{1,0:T(8,128)(2,1)S(1)}, bf16[2048,512]{1,0:T(8,128)(2,1)}, u32[]{:S(2)}) copy-start(bf16[2048,512]{1,0:T(8,128)(2,1)} %get-tuple-element.10) | copy-start | bytes 6291460
  191.5 2.3 %copy-start = (bf16[512,2048]{1,0:T(8,128)(2,1)S(1)}, bf16[512,2048]{1,0:T(8,128)(2,1)}, u32[]{:S(2)}) copy-start(bf16[512,2048]{1,0:T(8,128)(2,1)} %get-tuple-element.11) | copy-start | bytes 6291460

commit v4 on v3

--- a/solution.py
+++ b/solution.py
@@ -289,7 +289,7 @@
 
             if a == 1:
                 for i, j in enumerate(range(cuts[3], nu)):
-                    pl.when(w == min(1 + 4 * i, nu - 1))(functools.partial(fold_rows, j))
+                    pl.when(w == min(1 + 2 * i, nu - 1))(functools.partial(fold_rows, j))
 
         fold(a * nu + nu - 1)
 
@@ -312,7 +312,7 @@
     zwait(1, nz - 2)
     lcopies(1)[0].wait()
 
-    cuts = (nu // 4, 3 * nu // 8, 5 * nu // 8, 6 * nu // 8)
+    cuts = (nu // 8, nu // 4, 3 * nu // 8, nu // 2)
     produce(0)
     for j in range(cuts[0]):
         fold_rows(j)

time: 195 us -> 196 us (level)
  no operation moved by 1% of the time
where the time goes in v4:
time: 196 us
  Pallas kernels  187 us (95%)
  local copies, waits for them, and re-layouts  7.55 us (4%)
    pallas_call x1, Pallas kernels, local(): pl.pallas_call(functools.partial(kernel, nz, nd, fac), out_shape=(jax.Sha...  187 us
    unnamed x8, local copies, waits for them, and re-layouts  7.55 us

profile of v4, /device:TPU:0, one launch (start us, length us, event | category | flops | bytes accessed | tf_op | source)
XLA Modules:
  0.0 195.6 jit_solution(6380990213096238384)
XLA Ops:
  0.6 187.4 %mlp.1 = (bf16[512,512]{1,0:T(8,128)(2,1)}, bf16[512,512]{1,0:T(8,128)(2,1)}, bf16[2048,512]{1,0:T(8,128)(2,1)}, bf16[512,2048]{1,0:T(8,128)(2,1)}) custom-call(bf16[512,512]{1,0:T(8,128)(2,1)} %tok_in.1, bf16[2048,512]{1,0:T(8,128)(2,1)} %win_in.1, bf16[512,2048]{1,0:T(8,128)(2,1)} %wout_in.1, bf16[512,512]{1,0:T(8,128)(2,1)} %cot_in.1), custom_call_target="tpu_custom_call" | custom-call | flops 25769803776 | bytes 20971520 | tf_op jit(solution)/shard_map/mlp/pallas_call | solution.py:395
  188.1 0.0 copy-start.1
  188.1 2.0 %copy.12 = bf16[512,512]{1,0:T(8,128)(2,1)} copy(bf16[512,512]{1,0:T(8,128)(2,1)} %get-tuple-element.8) | data formatting | bytes 1048576
  190.1 1.9 copy.13
  191.9 0.0 copy-done.1
  192.0 0.0 copy-start
  192.0 1.3 copy.14
  193.3 1.0 copy-done
  194.3 1.3 copy.15
Async XLA Ops:
  188.1 3.9 %copy-start.1 = (bf16[2048,512]{1,0:T(8,128)(2,1)S(1)}, bf16[2048,512]{1,0:T(8,128)(2,1)}, u32[]{:S(2)}) copy-start(bf16[2048,512]{1,0:T(8,128)(2,1)} %get-tuple-element.10) | copy-start | bytes 6291460
  192.0 2.3 %copy-start = (bf16[512,2048]{1,0:T(8,128)(2,1)S(1)}, bf16[512,2048]{1,0:T(8,128)(2,1)}, u32[]{:S(2)}) copy-start(bf16[512,2048]{1,0:T(8,128)(2,1)} %get-tuple-element.11) | copy-start | bytes 6291460
